TPU v7x, 32 devices: a whole 2x2x4 slice. The times are simulated.
32 devices in a mesh: dp: 8 (over z, y), mp: 4 (over x, core).
Axes of the slice: x: 2, y: 2, z: 4, core: 2. Of those that a mesh axis runs over, the one named last changes fastest.
Arguments:
- block_input: bfloat16 [8, 2048, 768], P('dp', 'mp'), may hold values from -6 to 6
- out_cotangent: bfloat16 [8, 2048, 768], P('dp', 'mp'), may hold values from -6 to 6
- lengths: int32 [8], P('dp'), may hold values from 1024 to 2048, as said below
- w_qkv: float32 [768, 3, 768], P('dp', None, 'mp'), may hold values from -0.21875 to 0.21875
- w_out: float32 [768, 768], P('mp', 'dp'), may hold values from -1.75 to 1.75
- w_up: float32 [768, 3072], P('dp', 'mp'), may hold values from -0.21875 to 0.21875
- w_down: float32 [3072, 768], P('mp', 'dp'), may hold values from -0.109375 to 0.109375
- pair_bias: float32 [2048, 256], P(('dp', 'mp')), may hold values from -1.5 to 1.5
- norm_gains: float32 [2, 768], replicated, may hold values from 0.5 to 1.5
- first_qkv: float32 [768, 3, 768], P('dp', None, 'mp'), may hold values from -0.625 to 0.625
- first_out: float32 [768, 768], P('mp', 'dp'), may hold values from -0.125 to 0.125
- first_up: float32 [768, 3072], P('dp', 'mp'), may hold values from -0.625 to 0.625
- first_down: float32 [3072, 768], P('mp', 'dp'), may hold values from -0.625 to 0.625
- first_bias: float32 [2048, 256], P(('dp', 'mp')), may hold values from -0.03125 to 0.03125
- first_gains: float32 [2, 768], replicated, may hold values from -0.625 to 0.625
- second_qkv: float32 [768, 3, 768], P('dp', None, 'mp'), may hold values from 0.002 to 0.03
- second_out: float32 [768, 768], P('mp', 'dp'), may hold values from 0.0001 to 0.0015
- second_up: float32 [768, 3072], P('dp', 'mp'), may hold values from 0.002 to 0.03
- second_down: float32 [3072, 768], P('mp', 'dp'), may hold values from 0.002 to 0.03
- second_bias: float32 [2048, 256], P(('dp', 'mp')), may hold values from 5e-05 to 0.00075
- second_gains: float32 [2, 768], replicated, may hold values from 0.002 to 0.03
Outputs:
- block_output: bfloat16 [8, 2048, 768], P('dp', 'mp')
- grad_input: float32 [8, 2048, 768], P('dp', 'mp')
- grad_qkv: float32 [768, 3, 768], P('dp', None, 'mp')
- grad_out: float32 [768, 768], P('mp', 'dp')
- grad_up: float32 [768, 3072], P('dp', 'mp')
- grad_down: float32 [3072, 768], P('mp', 'dp')
- grad_bias: float32 [2048, 256], P(('dp', 'mp'))
- grad_gains: float32 [2, 768], replicated
- newfirst_qkv: float32 [768, 3, 768], P('dp', None, 'mp')
- newfirst_out: float32 [768, 768], P('mp', 'dp')
- newfirst_up: float32 [768, 3072], P('dp', 'mp')
- newfirst_down: float32 [3072, 768], P('mp', 'dp')
- newfirst_bias: float32 [2048, 256], P(('dp', 'mp'))
- newfirst_gains: float32 [2, 768], replicated
- newsecond_qkv: float32 [768, 3, 768], P('dp', None, 'mp')
- newsecond_out: float32 [768, 768], P('mp', 'dp')
- newsecond_up: float32 [768, 3072], P('dp', 'mp')
- newsecond_down: float32 [3072, 768], P('mp', 'dp')
- newsecond_bias: float32 [2048, 256], P(('dp', 'mp'))
- newsecond_gains: float32 [2, 768], replicated
- update_qkv: float32 [768, 3, 768], P('dp', None, 'mp')
- update_out: float32 [768, 768], P('mp', 'dp')
- update_up: float32 [768, 3072], P('dp', 'mp')
- update_down: float32 [3072, 768], P('mp', 'dp')
- update_bias: float32 [2048, 256], P(('dp', 'mp'))
- update_gains: float32 [2, 768], replicated
- rms_stats: float32 [3], replicated
Inputs may be any that keep to these rules, and one draw needn't show every extreme that they name: `lengths`: every length is at least half of 2048, and one of them is exactly 2048.
All inputs are finite; a program needn't handle non-finite values.
Results may differ from a plain program's by a relative error of at most 0.012.
Values may be sent and summed in bfloat16 or wider, within the bound.
A program may use at most 192 MiB of HBM per device.

v0:
```python
import jax
import jax.numpy as jnp
from jax import lax
from jax.sharding import PartitionSpec as P

LEN = 2048
ADAM_STEP = 10
EPS = 1e-06
BETA_ONE = 0.9
BETA_TWO = 0.99
LEARN_RATE = 0.03
WEIGHT_DECAY = 0.1
ADAM_EPS = 1e-08


def skew_band(bias_rows):
    height, width = bias_rows.shape
    padded = jnp.concatenate(
        [
            jnp.zeros((height, 1), bias_rows.dtype),
            bias_rows[:, ::-1],
            jnp.zeros((height, height), bias_rows.dtype),
        ],
        axis=1,
    )
    return padded.reshape(-1)[: height * (height + width)].reshape(height, height + width)


def unskew_band(band_grad, window):
    height, width = band_grad.shape
    flat = jnp.concatenate([band_grad.reshape(-1), jnp.zeros((height,), band_grad.dtype)])
    return flat.reshape(height, width + 1)[:, 1 : window + 1][:, ::-1]


def mix_forward(queries, key_rows, value_rows, bias_low):
    seq_len, channels = queries.shape
    window = bias_low.shape[1]
    block = min(512, seq_len)
    exp_keys = jnp.exp(key_rows)
    front = jnp.zeros((window, channels), jnp.bfloat16)
    keys_pad = jnp.concatenate([front, exp_keys.astype(jnp.bfloat16)], axis=0)
    product_pad = jnp.concatenate([front, (exp_keys * value_rows).astype(jnp.bfloat16)], axis=0)

    def one_block(block_index):
        offset = block_index * block
        band_rows = skew_band(lax.dynamic_slice_in_dim(bias_low, offset, block, 0))
        key_block = lax.dynamic_slice_in_dim(keys_pad, offset, block + window, 0)
        product_block = lax.dynamic_slice_in_dim(product_pad, offset, block + window, 0)
        numerator = jnp.dot(band_rows, product_block, preferred_element_type=jnp.float32)
        denominator = jnp.dot(band_rows, key_block, preferred_element_type=jnp.float32)
        return (numerator, denominator)

    numerator, denominator = lax.map(one_block, jnp.arange(seq_len // block, dtype=jnp.int32))
    return (
        numerator.reshape(seq_len, channels),
        denominator.reshape(seq_len, channels),
        keys_pad,
        product_pad,
    )


def mix_backward(
    queries,
    key_rows,
    value_rows,
    numerator,
    denominator,
    keys_pad,
    product_pad,
    bias_low,
    grad_mixed,
):
    seq_len, channels = queries.shape
    window = bias_low.shape[1]
    block = min(512, seq_len)
    gate_sig = jax.nn.sigmoid(queries)
    mixed_ratio = numerator / denominator
    grad_query = grad_mixed * mixed_ratio * gate_sig * (1.0 - gate_sig)
    grad_numerator = (grad_mixed * gate_sig / denominator).astype(jnp.bfloat16)
    grad_denominator = (-grad_mixed * gate_sig * mixed_ratio / denominator).astype(jnp.bfloat16)

    def one_block(carry, block_index):
        product_sum, key_sum = carry
        offset = block_index * block
        band_rows = skew_band(lax.dynamic_slice_in_dim(bias_low, offset, block, 0))
        key_block = lax.dynamic_slice_in_dim(keys_pad, offset, block + window, 0)
        product_block = lax.dynamic_slice_in_dim(product_pad, offset, block + window, 0)
        upper_block = lax.dynamic_slice_in_dim(grad_numerator, offset, block, 0)
        lower_block = lax.dynamic_slice_in_dim(grad_denominator, offset, block, 0)
        product_part = jnp.einsum(
            "ij,ic->jc", band_rows, upper_block, preferred_element_type=jnp.float32
        )
        key_part = jnp.einsum(
            "ij,ic->jc", band_rows, lower_block, preferred_element_type=jnp.float32
        )
        product_sum = lax.dynamic_update_slice_in_dim(
            product_sum,
            lax.dynamic_slice_in_dim(product_sum, offset, block + window, 0) + product_part,
            offset,
            0,
        )
        key_sum = lax.dynamic_update_slice_in_dim(
            key_sum,
            lax.dynamic_slice_in_dim(key_sum, offset, block + window, 0) + key_part,
            offset,
            0,
        )
        band_grad = jnp.einsum(
            "ic,jc->ij", upper_block, product_block, preferred_element_type=jnp.float32
        )
        band_grad = band_grad + jnp.einsum(
            "ic,jc->ij", lower_block, key_block, preferred_element_type=jnp.float32
        )
        return ((product_sum, key_sum), unskew_band(band_grad, window))

    zeros_pad = jnp.zeros((seq_len + window, channels), jnp.float32)
    sums_pad, bias_blocks = lax.scan(
        one_block, (zeros_pad, zeros_pad), jnp.arange(seq_len // block, dtype=jnp.int32)
    )
    exp_keys = jnp.exp(key_rows)
    grad_product = sums_pad[0][window:]
    grad_keyexp = sums_pad[1][window:] + grad_product * value_rows
    grad_value = grad_product * exp_keys
    grad_key = grad_keyexp * exp_keys
    return (grad_query, grad_key, grad_value, bias_blocks.reshape(seq_len, window))


def rms_rescale(inputs):
    return lax.rsqrt(jnp.mean(inputs * inputs, axis=-1, keepdims=True) + EPS)


def norm_back(inputs, rescale, gain, grad_normed):
    scaled = grad_normed * gain
    grad_inputs = rescale * scaled - inputs * rescale * rescale * rescale * jnp.mean(
        scaled * inputs, axis=-1, keepdims=True
    )
    grad_gain = jnp.sum(grad_normed * inputs * rescale, axis=(0, 1))
    return (grad_inputs, grad_gain)


def gelu_tanh(pre_act):
    return jax.nn.gelu(pre_act, approximate=True)


def adam_step(param, grad, first, second, step_value, decay):
    new_first = BETA_ONE * first + (1.0 - BETA_ONE) * grad
    new_second = BETA_TWO * second + (1.0 - BETA_TWO) * grad * grad
    first_hat = new_first / (1.0 - jnp.power(jnp.float32(BETA_ONE), step_value))
    second_hat = new_second / (1.0 - jnp.power(jnp.float32(BETA_TWO), step_value))
    update = -LEARN_RATE * (first_hat / (jnp.sqrt(second_hat) + ADAM_EPS) + decay * param)
    return (new_first, new_second, update)


def shards(
    block_input,
    out_cotangent,
    lengths,
    w_qkv,
    w_out,
    w_up,
    w_down,
    pair_bias,
    norm_gains,
    first_qkv,
    first_out,
    first_up,
    first_down,
    first_bias,
    first_gains,
    second_qkv,
    second_out,
    second_up,
    second_down,
    second_bias,
    second_gains,
):
    query_weights, mixer_weights, hidden_weights, back_weights = (
        lax.all_gather(w_qkv.astype(jnp.bfloat16), "dp", axis=0, tiled=True),
        lax.all_gather(w_out.astype(jnp.bfloat16), "dp", axis=1, tiled=True),
        lax.all_gather(w_up.astype(jnp.bfloat16), "dp", axis=0, tiled=True),
        lax.all_gather(w_down.astype(jnp.bfloat16), "dp", axis=1, tiled=True),
    )
    bias_full = lax.all_gather(pair_bias, ("dp", "mp"), axis=0, tiled=True)
    exp_bias = jnp.exp(bias_full)
    bias_low = exp_bias.astype(jnp.bfloat16)
    seqs, quarter, width = block_input.shape
    dp_count = lax.axis_size("dp")
    positions = lax.axis_index("mp") * quarter + jnp.arange(quarter, dtype=jnp.int32)
    valid_mask = (positions[None, :] < lengths[:, None]).astype(jnp.float32)
    input_float = block_input.astype(jnp.float32)
    rescale_one = rms_rescale(input_float)
    normed_one = (input_float * rescale_one * norm_gains[0]).astype(jnp.bfloat16)
    full_one = lax.all_gather(normed_one, "mp", axis=1, tiled=True)
    projected = jnp.einsum(
        "std,dkc->stkc", full_one, query_weights, preferred_element_type=jnp.float32
    )
    queries = projected[:, :, 0]
    key_rows = projected[:, :, 1]
    value_rows = projected[:, :, 2]
    numerator, denominator, keys_pad, product_pad = jax.vmap(mix_forward, in_axes=(0, 0, 0, None))(
        queries, key_rows, value_rows, bias_low
    )
    mixed_low = (jax.nn.sigmoid(queries) * numerator / denominator).astype(jnp.bfloat16)
    attn_terms = jnp.einsum(
        "stc,cd->std", mixed_low, mixer_weights, preferred_element_type=jnp.float32
    )
    attn_rows = lax.psum_scatter(attn_terms, "mp", scatter_dimension=1, tiled=True)
    resid = input_float + attn_rows
    rescale_two = rms_rescale(resid)
    normed_two = (resid * rescale_two * norm_gains[1]).astype(jnp.bfloat16)
    full_two = lax.all_gather(normed_two, "mp", axis=1, tiled=True)
    pre_act = jnp.einsum(
        "std,df->stf", full_two, hidden_weights, preferred_element_type=jnp.float32
    )
    act_low = gelu_tanh(pre_act).astype(jnp.bfloat16)
    ffn_terms = jnp.einsum("stf,fd->std", act_low, back_weights, preferred_element_type=jnp.float32)
    ffn_rows = lax.psum_scatter(
        ffn_terms.astype(jnp.bfloat16), "mp", scatter_dimension=1, tiled=True
    ).astype(jnp.float32)
    block_output = (resid + ffn_rows).astype(jnp.bfloat16)
    cotangent = out_cotangent.astype(jnp.float32) * valid_mask[:, :, None]
    cot_low = cotangent.astype(jnp.bfloat16)
    grad_full = lax.all_gather(cot_low, "mp", axis=1, tiled=True)
    grad_act = jnp.einsum(
        "std,fd->stf", grad_full, back_weights, preferred_element_type=jnp.float32
    )
    grad_pre = jax.vjp(gelu_tanh, pre_act)[1](grad_act)[0].astype(jnp.bfloat16)
    normed_terms = jnp.einsum(
        "stf,df->std", grad_pre, hidden_weights, preferred_element_type=jnp.float32
    )
    grad_normed_two = lax.psum_scatter(normed_terms, "mp", scatter_dimension=1, tiled=True)
    grad_up_local = jnp.einsum(
        "std,stf->df", full_two, grad_pre, preferred_element_type=jnp.float32
    )
    grad_down_local = jnp.einsum(
        "stf,std->fd", act_low, grad_full, preferred_element_type=jnp.float32
    )
    grad_resid_norm, gain_two_grad = norm_back(resid, rescale_two, norm_gains[1], grad_normed_two)
    grad_resid = cotangent + grad_resid_norm
    resid_full = lax.all_gather(grad_resid.astype(jnp.bfloat16), "mp", axis=1, tiled=True)
    grad_mixed = jnp.einsum(
        "std,cd->stc", resid_full, mixer_weights, preferred_element_type=jnp.float32
    )
    grad_mixer = jnp.einsum(
        "stc,std->cd", mixed_low, resid_full, preferred_element_type=jnp.float32
    )
    grad_query, grad_key, grad_value, bias_parts = jax.vmap(
        mix_backward, in_axes=(0, 0, 0, 0, 0, 0, 0, None, 0)
    )(
        queries,
        key_rows,
        value_rows,
        numerator,
        denominator,
        keys_pad,
        product_pad,
        bias_low,
        grad_mixed,
    )
    grad_bias_local = jnp.sum(bias_parts, axis=0) * exp_bias
    grad_proj = jnp.stack([grad_query, grad_key, grad_value], axis=2).astype(jnp.bfloat16)
    input_terms = jnp.einsum(
        "stkc,dkc->std", grad_proj, query_weights, preferred_element_type=jnp.float32
    )
    grad_normed_one = lax.psum_scatter(
        input_terms.astype(jnp.bfloat16), "mp", scatter_dimension=1, tiled=True
    ).astype(jnp.float32)
    grad_projection = jnp.einsum(
        "std,stkc->dkc", full_one, grad_proj, preferred_element_type=jnp.float32
    )
    grad_input_norm, gain_one_grad = norm_back(
        input_float, rescale_one, norm_gains[0], grad_normed_one
    )
    grad_input = grad_resid + grad_input_norm
    owned_qkv, owned_out, owned_up, owned_down = (
        lax.psum_scatter(grad_projection, "dp", scatter_dimension=0, tiled=True),
        lax.psum_scatter(grad_mixer, "dp", scatter_dimension=1, tiled=True),
        lax.psum_scatter(grad_up_local, "dp", scatter_dimension=0, tiled=True),
        lax.psum_scatter(grad_down_local, "dp", scatter_dimension=1, tiled=True),
    )
    owned_bias = lax.psum_scatter(grad_bias_local, ("dp", "mp"), scatter_dimension=0, tiled=True)
    mask_cols = valid_mask[:, :, None]
    local_sums = jnp.stack(
        [
            jnp.sum(mask_cols * input_float * input_float),
            jnp.sum(mask_cols * attn_rows * attn_rows),
            jnp.sum(mask_cols * ffn_rows * ffn_rows),
            jnp.sum(valid_mask),
        ]
    )
    gain_grads, global_sums = lax.psum(
        (jnp.stack([gain_one_grad, gain_two_grad]), local_sums), ("dp", "mp")
    )
    grad_scale = float(seqs * dp_count * LEN) ** (-0.5)
    scaled = [
        owned_qkv * grad_scale,
        owned_out * grad_scale,
        owned_up * grad_scale,
        owned_down * grad_scale,
        owned_bias * grad_scale,
        gain_grads * grad_scale,
    ]
    params = (w_qkv, w_out, w_up, w_down, pair_bias, norm_gains)
    firsts = (first_qkv, first_out, first_up, first_down, first_bias, first_gains)
    seconds = (second_qkv, second_out, second_up, second_down, second_bias, second_gains)
    decays = (WEIGHT_DECAY, WEIGHT_DECAY, WEIGHT_DECAY, WEIGHT_DECAY, 0.0, 0.0)
    step_value = jnp.float32(ADAM_STEP)
    states = [
        adam_step(
            params[place], scaled[place], firsts[place], seconds[place], step_value, decays[place]
        )
        for place in range(6)
    ]
    rms_stats = jnp.sqrt(global_sums[:3] / (global_sums[3] * width))
    return (
        block_output,
        grad_input,
        scaled[0],
        scaled[1],
        scaled[2],
        scaled[3],
        scaled[4],
        scaled[5],
        states[0][0],
        states[1][0],
        states[2][0],
        states[3][0],
        states[4][0],
        states[5][0],
        states[0][1],
        states[1][1],
        states[2][1],
        states[3][1],
        states[4][1],
        states[5][1],
        states[0][2],
        states[1][2],
        states[2][2],
        states[3][2],
        states[4][2],
        states[5][2],
        rms_stats,
    )


def solution(mesh):
    placed = (
        P("dp", "mp", None),
        P("dp", "mp", None),
        P("dp"),
        P("dp", None, "mp"),
        P("mp", "dp"),
        P("dp", "mp"),
        P("mp", "dp"),
        P(("dp", "mp"), None),
        P(),
        P("dp", None, "mp"),
        P("mp", "dp"),
        P("dp", "mp"),
        P("mp", "dp"),
        P(("dp", "mp"), None),
        P(),
        P("dp", None, "mp"),
        P("mp", "dp"),
        P("dp", "mp"),
        P("mp", "dp"),
        P(("dp", "mp"), None),
        P(),
    )
    return jax.shard_map(
        shards,
        mesh=mesh,
        in_specs=placed,
        out_specs=(
            P("dp", "mp", None),
            P("dp", "mp", None),
            P("dp", None, "mp"),
            P("mp", "dp"),
            P("dp", "mp"),
            P("mp", "dp"),
            P(("dp", "mp"), None),
            P(),
            P("dp", None, "mp"),
            P("mp", "dp"),
            P("dp", "mp"),
            P("mp", "dp"),
            P(("dp", "mp"), None),
            P(),
            P("dp", None, "mp"),
            P("mp", "dp"),
            P("dp", "mp"),
            P("mp", "dp"),
            P(("dp", "mp"), None),
            P(),
            P("dp", None, "mp"),
            P("mp", "dp"),
            P("dp", "mp"),
            P("mp", "dp"),
            P(("dp", "mp"), None),
            P(),
            P(),
        ),
        check_vma=False,
    )
```

profile of v0, /device:TPU:0, one launch (start us, length us, event | category | flops | bytes accessed | tf_op | source)
XLA Modules:
  0.0 1117.6 jit_solution(440134953824008164)
XLA Ops:
  13.6 40.4 %all_gather.28 = bf16[768,3,192]{2,1,0:T(4,128)(2,1)S(1)} all-gather(bf16[96,3,192]{2,1,0:T(4,128)(2,1)S(1)} %copy.88), channel_id=1, replica_groups=mesh['dp'=8,'mp'=4] {'dp'}, dimensions={0}, use_global_device_ids=true | all-gather | bytes 995328 | tf_op jit(solution)/shard_map/all_gather | solution.py:178
  55.0 31.3 %all_gather.30 = bf16[192,768]{0,1:T(8,128)(2,1)S(1)} all-gather(bf16[192,96]{0,1:T(8,128)(2,1)S(1)} %copy.94), channel_id=1, replica_groups=mesh['dp'=8,'mp'=4] {'dp'}, dimensions={1}, use_global_device_ids=true | all-gather | bytes 331776 | tf_op jit(solution)/shard_map/all_gather | solution.py:179
  89.2 16.2 %all-gather.8.cloned.1.call-done = bf16[1,2048,768]{2,1,0:T(8,128)(2,1)} async-done(((bf16[1,512,768]{2,1,0:T(8,128)(2,1)}), bf16[1,2048,768]{2,1,0:T(8,128)(2,1)}) %all-gather.8.cloned.1.call-update) | async-done | bytes 3145744 | tf_op jit(solution)/shard_map/all_gather | solution.py:193
  115.6 40.1 %while.36 = (s32[]{:T(128)}, f32[4,1,512,192]{2,3,1,0:T(8,128)}, f32[4,1,512,192]{2,3,1,0:T(8,128)}, s32[4]{0:T(128)S(1)}, bf16[2048,256]{1,0:T(8,128)(2,1)}, /*...) while((s32[]{:T(128)}, f32[4,1,512,192]{2,3,1,0:T(8,128)}, ...), condition=%wide.region_2.3_spmd, body=%wide.region_1.2_spmd.sunk | while | flops 304352256 | bytes 9974028 | solution.py:53
  170.2 56.4 %reduce-scatter.12.cloned.1.call-done = f32[1,512,768]{2,1,0:T(8,128)} async-done(((f32[1,2048,768]{2,1,0:T(8,128)}), f32[1,512,768]{2,1,0:T(8,128)}) %reduce-scatter.12.cloned.1.call-update) | async-done | bytes 1572880 | tf_op jit(solution)/shard_map/reduce_scatter | solution.py:207
  231.4 26.5 %all-gather.12.cloned.1.call-done = bf16[1,2048,768]{2,1,0:T(8,128)(2,1)} async-done(((bf16[1,512,768]{2,1,0:T(8,128)(2,1)}), bf16[1,2048,768]{2,1,0:T(8,128)(2,1)}) %all-gather.12.cloned.1.call-update) | async-done | bytes 3145744 | tf_op jit(solution)/shard_map/all_gather | solution.py:211
  265.4 22.4 %all-gather.18.cloned.1.call-done = bf16[1,2048,768]{2,1,0:T(8,128)(2,1)} async-done(((bf16[1,512,768]{2,1,0:T(8,128)(2,1)}), bf16[1,2048,768]{2,1,0:T(8,128)(2,1)}) %all-gather.18.cloned.1.call-update) | async-done | bytes 3145744 | tf_op jit(solution)/shard_map/all_gather | solution.py:223
  296.1 69.1 %reduce-scatter.24.cloned.1.call-done = f32[768,96]{0,1:T(8,128)} async-done(((f32[768,768]{0,1:T(8,128)}), f32[768,96]{0,1:T(8,128)}) %reduce-scatter.24.cloned.1.call-update) | async-done | bytes 294928 | tf_op jit(solution)/shard_map/reduce_scatter | solution.py:279
  367.5 41.4 %all-gather.16.cloned.1.call-done = bf16[768,768]{0,1:T(8,128)(2,1)} async-done(((bf16[768,96]{0,1:T(8,128)(2,1)}), bf16[768,768]{0,1:T(8,128)(2,1)}) %all-gather.16.cloned.1.call-update) | async-done | bytes 1179664 | tf_op jit(solution)/shard_map/all_gather | solution.py:181
  408.9 8.2 fusion.37
  424.7 8.5 fusion.54
  433.3 47.0 %reduce-scatter.16.cloned.1.call-done = f32[1,512,768]{2,1,0:T(8,128)} async-done(((f32[1,2048,768]{2,1,0:T(8,128)}), f32[1,512,768]{2,1,0:T(8,128)}) %reduce-scatter.16.cloned.1.call-update) | async-done | bytes 1572880 | tf_op jit(solution)/shard_map/reduce_scatter | solution.py:231
  482.7 37.9 %reduce-scatter.14.cloned.1.call-done = bf16[1,512,768]{2,1,0:T(8,128)(2,1)} async-done(((bf16[1,2048,768]{2,1,0:T(8,128)(2,1)}), bf16[1,512,768]{2,1,0:T(8,128)(2,1)}) %reduce-scatter.14.cloned.1.call-update) | async-done | bytes 786448 | tf_op jit(solution)/shard_map/reduce_scatter | solution.py:217
  538.3 16.3 %all-gather.20.cloned.1.call-done = bf16[1,2048,768]{2,1,0:T(8,128)(2,1)} async-done(((bf16[1,512,768]{2,1,0:T(8,128)(2,1)}), bf16[1,2048,768]{2,1,0:T(8,128)(2,1)}) %all-gather.20.cloned.1.call-update) | async-done | bytes 3145744 | tf_op jit(solution)/shard_map/all_gather | solution.py:240
  565.5 186.5 %while.37 = (s32[]{:T(128)}, f32[1,2304,192]{1,2,0:T(8,128)}, f32[1,2304,192]{1,2,0:T(8,128)}, f32[4,1,512,256]{3,2,1,0:T(8,128)}, s32[4]{0:T(128)S(1)}, /*index...) while((s32[]{:T(128)}, f32[1,2304,192]{1,2,0:T(8,128)}, ...), condition=%wide.region_10.11_spmd, body=%wide.region_8.10_spmd.sunk | while | flops 607325184 | bytes 47336400 | solution.py:117
  572.2 16.3 %pad_reduce_fusion.2 = f32[393728]{0:T(1024)S(1)} fusion(f32[1,393216]{1,0:T(1,128)S(1)} %bitcast.305), kind=kLoop, calls=%fused_computation.13.clone.1 | loop fusion | bytes 3147776 | tf_op jit(solution)/shard_map/vmap()/while/body/eval_jaxpr/concatenate | solution.py:31
  619.6 16.3 %pad_reduce_fusion.2 = f32[393728]{0:T(1024)S(1)} fusion(f32[1,393216]{1,0:T(1,128)S(1)} %bitcast.305), kind=kLoop, calls=%fused_computation.13.clone.1 | loop fusion | bytes 3147776 | tf_op jit(solution)/shard_map/vmap()/while/body/eval_jaxpr/concatenate | solution.py:31
  667.0 16.3 %pad_reduce_fusion.2 = f32[393728]{0:T(1024)S(1)} fusion(f32[1,393216]{1,0:T(1,128)S(1)} %bitcast.305), kind=kLoop, calls=%fused_computation.13.clone.1 | loop fusion | bytes 3147776 | tf_op jit(solution)/shard_map/vmap()/while/body/eval_jaxpr/concatenate | solution.py:31
  713.6 16.3 %pad_reduce_fusion.2 = f32[393728]{0:T(1024)S(1)} fusion(f32[1,393216]{1,0:T(1,128)S(1)} %bitcast.305), kind=kLoop, calls=%fused_computation.13.clone.1 | loop fusion | bytes 3147776 | tf_op jit(solution)/shard_map/vmap()/while/body/eval_jaxpr/concatenate | solution.py:31
  775.8 38.9 %reduce-scatter.28.cloned.1.call-done = f32[96,192]{1,0:T(8,128)} async-done(((f32[768,192]{1,0:T(8,128)}), f32[96,192]{1,0:T(8,128)}) %reduce-scatter.28.cloned.1.call-update) | async-done | bytes 73744
  816.5 69.8 %reduce-scatter.20.cloned.1.call-done = f32[96,3,192]{2,0,1:T(8,128)} async-done(((f32[768,3,192]{2,0,1:T(8,128)}), f32[96,3,192]{2,0,1:T(8,128)}) %reduce-scatter.20.cloned.1.call-update) | async-done | bytes 221200 | tf_op jit(solution)/shard_map/reduce_scatter | solution.py:276
  888.5 135.4 %reduce-scatter.26.cloned.1.call-done = f32[64,256]{1,0:T(8,128)} async-done(((f32[2048,256]{1,0:T(8,128)}), f32[64,256]{1,0:T(8,128)}) %reduce-scatter.26.cloned.1.call-update) | async-done | bytes 65552 | tf_op jit(solution)/shard_map/reduce_scatter | solution.py:281
  1025.4 34.9 %reduce-scatter.18.cloned.1.call-done = bf16[1,512,768]{2,1,0:T(8,128)(2,1)} async-done(((bf16[1,2048,768]{2,1,0:T(8,128)(2,1)}), bf16[1,512,768]{2,1,0:T(8,128)(2,1)}) %reduce-scatter.18.cloned.1.call-update) | async-done | bytes 786448 | tf_op jit(solution)/shard_map/reduce_scatter | solution.py:265
  1065.7 39.4 %all-reduce.3 = (f32[2,768]{1,0:T(2,128)S(1)}, f32[4]{0:T(128)S(1)}) all-reduce(f32[2,768]{1,0:T(2,128)S(1)} %pad_maximum_fusion.3, f32[4]{0:T(128)S(1)} %pad_maximum_fusion.4), channel_id=1, replica_groups=mesh['dp'=8,'mp'=4] {'dp','mp'}, use_global_device_ids=true, to_apply=%region_20.21 | all-reduce | flops 1540 | bytes 12320 | tf_op jit(solution)/shard_map/psum | solution.py:291
  (375 shorter events, 288.6 us)
Async XLA Ops:
  8.0 78.3 %all-gather.10.cloned.1.call-start = ((), (), s32[]{:S(2)}) async-start(), calls=%async_computation.10 | async-start | bytes 2162688 | tf_op jit(solution)/shard_map/all_gather | solution.py:183
  8.8 96.6 %all-gather.8.cloned.1.call-start = ((), (), s32[]{:S(2)}) async-start(), calls=%async_computation.9 | async-start | bytes 3932160 | tf_op jit(solution)/shard_map/all_gather | solution.py:193
  13.4 213.3 %reduce-scatter.12.cloned.1.call-start = ((), (), s32[]{:S(2)}) async-start(), calls=%async_computation.11 | async-start | bytes 7864320 | tf_op jit(solution)/shard_map/reduce_scatter | solution.py:207
  168.0 63.3 %all-gather.14.cloned.1.call-start = ((), (), s32[]{:S(2)}) async-start(), calls=%async_computation.13 | async-start | bytes 1327104 | tf_op jit(solution)/shard_map/all_gather | solution.py:180
  169.7 88.2 %all-gather.12.cloned.1.call-start = ((), (), s32[]{:S(2)}) async-start(), calls=%async_computation.12 | async-start | bytes 3932160 | tf_op jit(solution)/shard_map/all_gather | solution.py:211
  229.4 58.4 %all-gather.18.cloned.1.call-start = ((), (), s32[]{:S(2)}) async-start(), calls=%async_computation.16 | async-start | bytes 3932160 | tf_op jit(solution)/shard_map/all_gather | solution.py:223
  231.3 133.9 %reduce-scatter.24.cloned.1.call-start = ((), (), s32[]{:S(2)}) async-start(), calls=%async_computation.22 | async-start | bytes 2654208 | tf_op jit(solution)/shard_map/reduce_scatter | solution.py:279
  296.1 112.8 %all-gather.16.cloned.1.call-start = ((), (), s32[]{:S(2)}) async-start(), calls=%async_computation.14 | async-start | bytes 1327104 | tf_op jit(solution)/shard_map/all_gather | solution.py:181
  367.4 112.9 %reduce-scatter.16.cloned.1.call-start = ((), (), s32[]{:S(2)}) async-start(), calls=%async_computation.17 | async-start | bytes 7864320 | tf_op jit(solution)/shard_map/reduce_scatter | solution.py:231
  423.5 97.1 %reduce-scatter.14.cloned.1.call-start = ((), (), s32[]{:S(2)}) async-start(), calls=%async_computation.15 | async-start | bytes 3932160 | tf_op jit(solution)/shard_map/reduce_scatter | solution.py:217
  433.3 121.3 %all-gather.20.cloned.1.call-start = ((), (), s32[]{:S(2)}) async-start(), calls=%async_computation.18 | async-start | bytes 3932160 | tf_op jit(solution)/shard_map/all_gather | solution.py:240
  525.9 247.3 %reduce-scatter.22.cloned.1.call-start = ((), (), s32[]{:S(2)}) async-start(), calls=%async_computation.21 | async-start | bytes 2654208 | tf_op jit(solution)/shard_map/reduce_scatter | solution.py:278
  538.2 276.5 %reduce-scatter.28.cloned.1.call-start = ((), (), s32[]{:S(2)}) async-start(), calls=%async_computation.24 | async-start | bytes 884736
  752.0 134.3 %reduce-scatter.20.cloned.1.call-start = ((), (), s32[]{:S(2)}) async-start(), calls=%async_computation.20 | async-start | bytes 2654208 | tf_op jit(solution)/shard_map/reduce_scatter | solution.py:276
  760.9 262.9 %reduce-scatter.26.cloned.1.call-start = ((), (), s32[]{:S(2)}) async-start(), calls=%async_computation.23 | async-start | bytes 2162688 | tf_op jit(solution)/shard_map/reduce_scatter | solution.py:281
  765.8 294.6 %reduce-scatter.18.cloned.1.call-start = ((), (), s32[]{:S(2)}) async-start(), calls=%async_computation.19 | async-start | bytes 3932160 | tf_op jit(solution)/shard_map/reduce_scatter | solution.py:265
  815.7 208.1 %copy-start.34 = (f32[64,256]{1,0:T(8,128)S(1)}, f32[64,256]{1,0:T(8,128)}, u32[]{:S(2)}) copy-start(f32[64,256]{1,0:T(8,128)} %param.36) | copy-start | bytes 196612
  816.5 243.8 %copy-start.3 = (bf16[1,512,768]{2,1,0:T(8,128)(2,1)S(1)}, bf16[1,512,768]{2,1,0:T(8,128)(2,1)}, u32[]{:S(2)}) copy-start(bf16[1,512,768]{2,1,0:T(8,128)(2,1)} %param.29) | copy-start | bytes 2359300
  816.5 243.8 %copy-start.38 = (f32[768]{0:T(1024)S(1)}, f32[768]{0:T(1024)}, u32[]{:S(2)}) copy-start(f32[768]{0:T(1024)} %copy-done.37) | copy-start | bytes 9220
  816.5 243.8 %copy-start.42 = (f32[512]{0:T(512)S(1)}, f32[512]{0:T(512)}, u32[]{:S(2)}) copy-start(f32[512]{0:T(512)} %copy-done.41) | copy-start | bytes 6148
  888.5 218.3 %copy-start.43 = (f32[2,768]{1,0:T(2,128)S(1)}, f32[2,768]{1,0:T(2,128)}, u32[]{:S(2)}) copy-start(f32[2,768]{1,0:T(2,128)} %param.37) | copy-start | bytes 18436
  888.5 218.3 %copy-start.46 = (f32[2,768]{1,0:T(2,128)S(1)}, f32[2,768]{1,0:T(2,128)}, u32[]{:S(2)}) copy-start(f32[2,768]{1,0:T(2,128)} %param.49) | copy-start | bytes 18436
  888.5 218.3 %copy-start.47 = (f32[2,768]{1,0:T(2,128)S(1)}, f32[2,768]{1,0:T(2,128)}, u32[]{:S(2)}) copy-start(f32[2,768]{1,0:T(2,128)} %param.43) | copy-start | bytes 18436
  888.5 219.0 %copy-start.7 = (f32[1,512,768]{2,1,0:T(8,128)S(1)}, f32[1,512,768]{2,1,0:T(8,128)}, u32[]{:S(2)}) copy-start(f32[1,512,768]{2,1,0:T(8,128)} %get-tuple-element.374) | copy-start | bytes 4718596
  (54 other events, 1479.9 us)
Sparse Core Ops, SparseCore 0:
  11.7 63.4 all-gather.9
  77.4 27.9 all-gather.7
  168.2 58.4 reduce-scatter.11
  526.0 28.5 all-gather.19
Sparse Core Ops, SparseCore 1:
  171.3 41.5 all-gather.13
  229.5 28.3 all-gather.11
  259.4 28.3 all-gather.17
  296.2 69.0 reduce-scatter.23
  368.2 40.6 all-gather.15
  423.6 56.7 reduce-scatter.15
  482.7 37.8 reduce-scatter.13
  538.3 69.0 reduce-scatter.21
  752.1 62.5 reduce-scatter.27
  818.2 68.1 reduce-scatter.19
  888.5 135.3 reduce-scatter.25
  1026.6 33.7 reduce-scatter.17
where the time goes:
time: 1130 us; the launch traced here: 1120 us
  waiting for transfers between devices  613 us (54%)
  local copies, waits for them, and re-layouts  194 us (17%)
  matrix products  119 us (11%)
  blocking collectives  111 us (10%)
  other arithmetic  54.9 us (5%)
  between operations  17.4 us (2%)
    reduce_scatter x1, waiting for transfers between devices, shards(): lax.psum_scatter(grad_bias_local, ('dp', 'mp'), scatter_dimension=0, tile...  135 us
    reduce_scatter x1, waiting for transfers between devices, shards(): lax.psum_scatter(grad_projection, 'dp', scatter_dimension=0, tiled=True)  69.8 us
    reduce_scatter x1, waiting for transfers between devices, shards(): lax.psum_scatter(grad_down_local, 'dp', scatter_dimension=1, tiled=True)  69.1 us
    concatenate x4, local copies, waits for them, and re-layouts, unskew_band(): jnp.concatenate([band_grad.reshape(-1), jnp.zeros((height,), band_grad.dt...  65 us
    reduce_scatter x1, waiting for transfers between devices, shards(): lax.psum_scatter(attn_terms, 'mp', scatter_dimension=1, tiled=True)  56.4 us
    reduce_scatter x1, waiting for transfers between devices, shards(): lax.psum_scatter(normed_terms, 'mp', scatter_dimension=1, tiled=True)  47 us
    all_gather x1, waiting for transfers between devices, shards(): lax.all_gather(w_down.astype(jnp.bfloat16), 'dp', axis=1, tiled=True)  41.4 us
    all_gather x1, blocking collectives, shards(): lax.all_gather(w_qkv.astype(jnp.bfloat16), 'dp', axis=0, tiled=True)  40.4 us
  transfers between devices with their start and end apart: 16, of which 13 were waited for; matrix products, arithmetic and copies ran while one was open for 23% of the time, Pallas kernels for 0%

commit v1 on v0

--- a/solution.py
+++ b/solution.py
@@ -11,6 +11,22 @@
 LEARN_RATE = 0.03
 WEIGHT_DECAY = 0.1
 ADAM_EPS = 1e-08
+
+
+def ring_gather(x, axis, dim):
+    ways, here, step = (lax.axis_size(axis), lax.axis_index(axis), x.shape[dim])
+    shape = [n * ways if d == dim else n for d, n in enumerate(x.shape)]
+    full = lax.dynamic_update_slice_in_dim(jnp.zeros(shape, x.dtype), x, here * step, axis=dim)
+    going_up = going_down = x
+    for far in range(1, ways // 2 + 1):
+        going_up = lax.ppermute(going_up, axis, [(d, (d + 1) % ways) for d in range(ways)])
+        full = lax.dynamic_update_slice_in_dim(full, going_up, (here - far) % ways * step, axis=dim)
+        if 2 * far < ways:
+            going_down = lax.ppermute(going_down, axis, [(d, (d - 1) % ways) for d in range(ways)])
+            full = lax.dynamic_update_slice_in_dim(
+                full, going_down, (here + far) % ways * step, axis=dim
+            )
+    return full
 
 
 def skew_band(bias_rows):
@@ -175,7 +191,7 @@
     second_gains,
 ):
     query_weights, mixer_weights, hidden_weights, back_weights = (
-        lax.all_gather(w_qkv.astype(jnp.bfloat16), "dp", axis=0, tiled=True),
+        ring_gather(w_qkv.astype(jnp.bfloat16), "dp", 0),
         lax.all_gather(w_out.astype(jnp.bfloat16), "dp", axis=1, tiled=True),
         lax.all_gather(w_up.astype(jnp.bfloat16), "dp", axis=0, tiled=True),
         lax.all_gather(w_down.astype(jnp.bfloat16), "dp", axis=1, tiled=True),

time: 1130 us -> 1120 us (level)
  blocking collectives: 111 us -> 75.4 us
  starting transfers between devices: 1.33 us -> 18.5 us
    all_gather x1 -> x0, blocking collectives: 40.4 us -> none  [shards(): lax.all_gather(w_qkv.astype(jnp.bfloat16), 'dp', axis=0, tiled=True)]
    ppermute x0 -> x7, starting transfers between devices: none -> 17.3 us  [the longest x3 12.5 us: ring_gather(): lax.ppermute(going_down, axis, [(d, (d - 1) % ways) for d in range(ways)])]
  transfers between devices with their start and end apart: 16 -> 23, of which waited for: 13 -> 16; matrix products, arithmetic and copies ran while one was open for 23% -> 24% of each run, Pallas kernels for 0% -> 0%
where the time goes in v1:
time: 1120 us
  waiting for transfers between devices  620 us (55%)
  local copies, waits for them, and re-layouts  203 us (18%)
  matrix products  119 us (11%)
  blocking collectives  75.4 us (7%)
  other arithmetic  55.1 us (5%)
  starting transfers between devices  18.5 us (2%)
  between operations  17.7 us (2%)
    reduce_scatter x1, waiting for transfers between devices, shards(): lax.psum_scatter(grad_bias_local, ('dp', 'mp'), scatter_dimension=0, tile...  136 us
    reduce_scatter x1, waiting for transfers between devices, shards(): lax.psum_scatter(grad_projection, 'dp', scatter_dimension=0, tiled=True)  69.6 us
    reduce_scatter x1, waiting for transfers between devices, shards(): lax.psum_scatter(grad_down_local, 'dp', scatter_dimension=1, tiled=True)  69.1 us
    concatenate x4, local copies, waits for them, and re-layouts, unskew_band(): jnp.concatenate([band_grad.reshape(-1), jnp.zeros((height,), band_grad.dt...  65 us
    reduce_scatter x1, waiting for transfers between devices, shards(): lax.psum_scatter(attn_terms, 'mp', scatter_dimension=1, tiled=True)  56.9 us
    reduce_scatter x1, waiting for transfers between devices, shards(): lax.psum_scatter(normed_terms, 'mp', scatter_dimension=1, tiled=True)  47 us
    all_gather x1, waiting for transfers between devices, shards(): lax.all_gather(w_down.astype(jnp.bfloat16), 'dp', axis=1, tiled=True)  41.4 us
    unnamed x17, waiting for transfers between devices  39.8 us
  transfers between devices with their start and end apart: 23, of which 16 were waited for; matrix products, arithmetic and copies ran while one was open for 24% of the time, Pallas kernels for 0%

profile of v1, /device:TPU:0, one launch (start us, length us, event | category | flops | bytes accessed | tf_op | source)
XLA Modules:
  0.0 1115.8 jit_solution(594434238190717274)
XLA Ops:
  39.8 36.0 %all_gather.26 = bf16[192,768]{0,1:T(8,128)(2,1)S(1)} all-gather(bf16[192,96]{0,1:T(8,128)(2,1)S(1)} %copy.97), channel_id=1, replica_groups=mesh['dp'=8,'mp'=4] {'dp'}, dimensions={1}, use_global_device_ids=true | all-gather | bytes 331776 | tf_op jit(solution)/shard_map/all_gather | solution.py:195
  88.4 14.6 %all-gather.8.cloned.1.call-done = bf16[1,2048,768]{2,1,0:T(8,128)(2,1)} async-done(((bf16[1,512,768]{2,1,0:T(8,128)(2,1)}), bf16[1,2048,768]{2,1,0:T(8,128)(2,1)}) %all-gather.8.cloned.1.call-update) | async-done | bytes 3145744 | tf_op jit(solution)/shard_map/all_gather | solution.py:209
  113.2 40.6 %while.36 = (s32[]{:T(128)}, f32[4,1,512,192]{2,3,1,0:T(8,128)}, f32[4,1,512,192]{2,3,1,0:T(8,128)}, s32[4]{0:T(128)S(1)}, bf16[2048,256]{1,0:T(8,128)(2,1)}, /*...) while((s32[]{:T(128)}, f32[4,1,512,192]{2,3,1,0:T(8,128)}, ...), condition=%wide.region_2.3_spmd, body=%wide.region_1.2_spmd.sunk | while | flops 304352256 | bytes 9974028 | solution.py:69
  167.8 56.9 %reduce-scatter.12.cloned.1.call-done = f32[1,512,768]{2,1,0:T(8,128)} async-done(((f32[1,2048,768]{2,1,0:T(8,128)}), f32[1,512,768]{2,1,0:T(8,128)}) %reduce-scatter.12.cloned.1.call-update) | async-done | bytes 1572880 | tf_op jit(solution)/shard_map/reduce_scatter | solution.py:223
  229.6 26.4 %all-gather.12.cloned.1.call-done = bf16[1,2048,768]{2,1,0:T(8,128)(2,1)} async-done(((bf16[1,512,768]{2,1,0:T(8,128)(2,1)}), bf16[1,2048,768]{2,1,0:T(8,128)(2,1)}) %all-gather.12.cloned.1.call-update) | async-done | bytes 3145744 | tf_op jit(solution)/shard_map/all_gather | solution.py:227
  263.5 22.4 %all-gather.18.cloned.1.call-done = bf16[1,2048,768]{2,1,0:T(8,128)(2,1)} async-done(((bf16[1,512,768]{2,1,0:T(8,128)(2,1)}), bf16[1,2048,768]{2,1,0:T(8,128)(2,1)}) %all-gather.18.cloned.1.call-update) | async-done | bytes 3145744 | tf_op jit(solution)/shard_map/all_gather | solution.py:239
  285.9 8.3 fusion.44
  294.3 69.1 %reduce-scatter.24.cloned.1.call-done = f32[768,96]{0,1:T(8,128)} async-done(((f32[768,768]{0,1:T(8,128)}), f32[768,96]{0,1:T(8,128)}) %reduce-scatter.24.cloned.1.call-update) | async-done | bytes 294928 | tf_op jit(solution)/shard_map/reduce_scatter | solution.py:295
  365.6 41.4 %all-gather.16.cloned.1.call-done = bf16[768,768]{0,1:T(8,128)(2,1)} async-done(((bf16[768,96]{0,1:T(8,128)(2,1)}), bf16[768,768]{0,1:T(8,128)(2,1)}) %all-gather.16.cloned.1.call-update) | async-done | bytes 1179664 | tf_op jit(solution)/shard_map/all_gather | solution.py:197
  407.0 8.2 fusion.37
  422.9 8.5 fusion.54
  431.5 47.0 %reduce-scatter.16.cloned.1.call-done = f32[1,512,768]{2,1,0:T(8,128)} async-done(((f32[1,2048,768]{2,1,0:T(8,128)}), f32[1,512,768]{2,1,0:T(8,128)}) %reduce-scatter.16.cloned.1.call-update) | async-done | bytes 1572880 | tf_op jit(solution)/shard_map/reduce_scatter | solution.py:247
  480.9 37.8 %reduce-scatter.14.cloned.1.call-done = bf16[1,512,768]{2,1,0:T(8,128)(2,1)} async-done(((bf16[1,2048,768]{2,1,0:T(8,128)(2,1)}), bf16[1,512,768]{2,1,0:T(8,128)(2,1)}) %reduce-scatter.14.cloned.1.call-update) | async-done | bytes 786448 | tf_op jit(solution)/shard_map/reduce_scatter | solution.py:233
  536.4 16.4 %all-gather.20.cloned.1.call-done = bf16[1,2048,768]{2,1,0:T(8,128)(2,1)} async-done(((bf16[1,512,768]{2,1,0:T(8,128)(2,1)}), bf16[1,2048,768]{2,1,0:T(8,128)(2,1)}) %all-gather.20.cloned.1.call-update) | async-done | bytes 3145744 | tf_op jit(solution)/shard_map/all_gather | solution.py:256
  563.7 186.3 %while.37 = (s32[]{:T(128)}, f32[1,2304,192]{1,2,0:T(8,128)}, f32[1,2304,192]{1,2,0:T(8,128)}, f32[4,1,512,256]{3,2,1,0:T(8,128)}, s32[4]{0:T(128)S(1)}, /*index...) while((s32[]{:T(128)}, f32[1,2304,192]{1,2,0:T(8,128)}, ...), condition=%wide.region_10.11_spmd, body=%wide.region_8.10_spmd.sunk | while | flops 607325184 | bytes 47336400 | solution.py:133
  570.2 16.3 %pad_reduce_fusion.2 = f32[393728]{0:T(1024)S(1)} fusion(f32[1,393216]{1,0:T(1,128)S(1)} %bitcast.305), kind=kLoop, calls=%fused_computation.13.clone.1 | loop fusion | bytes 3147776 | tf_op jit(solution)/shard_map/vmap()/while/body/eval_jaxpr/concatenate | solution.py:47
  617.5 16.3 %pad_reduce_fusion.2 = f32[393728]{0:T(1024)S(1)} fusion(f32[1,393216]{1,0:T(1,128)S(1)} %bitcast.305), kind=kLoop, calls=%fused_computation.13.clone.1 | loop fusion | bytes 3147776 | tf_op jit(solution)/shard_map/vmap()/while/body/eval_jaxpr/concatenate | solution.py:47
  664.9 16.3 %pad_reduce_fusion.2 = f32[393728]{0:T(1024)S(1)} fusion(f32[1,393216]{1,0:T(1,128)S(1)} %bitcast.305), kind=kLoop, calls=%fused_computation.13.clone.1 | loop fusion | bytes 3147776 | tf_op jit(solution)/shard_map/vmap()/while/body/eval_jaxpr/concatenate | solution.py:47
  711.5 16.3 %pad_reduce_fusion.2 = f32[393728]{0:T(1024)S(1)} fusion(f32[1,393216]{1,0:T(1,128)S(1)} %bitcast.305), kind=kLoop, calls=%fused_computation.13.clone.1 | loop fusion | bytes 3147776 | tf_op jit(solution)/shard_map/vmap()/while/body/eval_jaxpr/concatenate | solution.py:47
  773.9 38.9 %reduce-scatter.28.cloned.1.call-done = f32[96,192]{1,0:T(8,128)} async-done(((f32[768,192]{1,0:T(8,128)}), f32[96,192]{1,0:T(8,128)}) %reduce-scatter.28.cloned.1.call-update) | async-done | bytes 73744
  814.6 69.6 %reduce-scatter.20.cloned.1.call-done = f32[96,3,192]{2,0,1:T(8,128)} async-done(((f32[768,3,192]{2,0,1:T(8,128)}), f32[96,3,192]{2,0,1:T(8,128)}) %reduce-scatter.20.cloned.1.call-update) | async-done | bytes 221200 | tf_op jit(solution)/shard_map/reduce_scatter | solution.py:292
  886.4 135.7 %reduce-scatter.26.cloned.1.call-done = f32[64,256]{1,0:T(8,128)} async-done(((f32[2048,256]{1,0:T(8,128)}), f32[64,256]{1,0:T(8,128)}) %reduce-scatter.26.cloned.1.call-update) | async-done | bytes 65552 | tf_op jit(solution)/shard_map/reduce_scatter | solution.py:297
  1023.6 34.9 %reduce-scatter.18.cloned.1.call-done = bf16[1,512,768]{2,1,0:T(8,128)(2,1)} async-done(((bf16[1,2048,768]{2,1,0:T(8,128)(2,1)}), bf16[1,512,768]{2,1,0:T(8,128)(2,1)}) %reduce-scatter.18.cloned.1.call-update) | async-done | bytes 786448 | tf_op jit(solution)/shard_map/reduce_scatter | solution.py:281
  1063.8 39.4 %all-reduce.3 = (f32[2,768]{1,0:T(2,128)S(1)}, f32[4]{0:T(128)S(1)}) all-reduce(f32[2,768]{1,0:T(2,128)S(1)} %pad_maximum_fusion.3, f32[4]{0:T(128)S(1)} %pad_maximum_fusion.4), channel_id=1, replica_groups=mesh['dp'=8,'mp'=4] {'dp','mp'}, use_global_device_ids=true, to_apply=%region_20.21 | all-reduce | flops 1540 | bytes 12320 | tf_op jit(solution)/shard_map/psum | solution.py:307
  (403 shorter events, 314.8 us)
Async XLA Ops:
  8.0 77.3 %all-gather.10.cloned.1.call-start = ((), (), s32[]{:S(2)}) async-start(), calls=%async_computation.10 | async-start | bytes 2162688 | tf_op jit(solution)/shard_map/all_gather | solution.py:199
  8.8 94.2 %all-gather.8.cloned.1.call-start = ((), (), s32[]{:S(2)}) async-start(), calls=%async_computation.9 | async-start | bytes 3932160 | tf_op jit(solution)/shard_map/all_gather | solution.py:209
  13.4 211.3 %reduce-scatter.12.cloned.1.call-start = ((), (), s32[]{:S(2)}) async-start(), calls=%async_computation.11 | async-start | bytes 7864320 | tf_op jit(solution)/shard_map/reduce_scatter | solution.py:223
  13.5 10.0 collective-permute-start
  16.5 8.7 collective-permute-start.1
  23.5 8.3 collective-permute-start.2
  25.3 7.7 collective-permute-start.3
  31.8 7.9 collective-permute-start.4
  33.0 50.0 %collective-permute-start.5 = (bf16[96,3,192]{2,0,1:T(8,128)(2,1)S(1)}, bf16[96,3,192]{2,0,1:T(8,128)(2,1)S(1)}, u32[]{:S(2)}, u32[]{:S(2)}) collective-permute-start(bf16[96,3,192]{2,0,1:T(8,128)(2,1)S(1)} %collective-permute-done.3), channel_id=1, source_target_pairs={{0,28},{4,0},{8,4},{12,8},{16,12},{20,16},{24,20},{28,24},{1,29},{... | collective-permute-start | bytes 331784 | tf_op jit(solution)/shard_map/ppermute | solution.py:25
  39.8 44.7 %collective-permute-start.6 = (bf16[96,3,192]{2,0,1:T(8,128)(2,1)S(1)}, bf16[96,3,192]{2,0,1:T(8,128)(2,1)S(1)}, u32[]{:S(2)}, u32[]{:S(2)}) collective-permute-start(bf16[96,3,192]{2,0,1:T(8,128)(2,1)S(1)} %collective-permute-done.4), channel_id=1, source_target_pairs={{0,4},{4,8},{8,12},{12,16},{16,20},{20,24},{24,28},{28,0},{1,5},{5... | collective-permute-start | bytes 331784 | tf_op jit(solution)/shard_map/ppermute | solution.py:22
  166.1 63.5 %all-gather.14.cloned.1.call-start = ((), (), s32[]{:S(2)}) async-start(), calls=%async_computation.13 | async-start | bytes 1327104 | tf_op jit(solution)/shard_map/all_gather | solution.py:196
  167.8 88.2 %all-gather.12.cloned.1.call-start = ((), (), s32[]{:S(2)}) async-start(), calls=%async_computation.12 | async-start | bytes 3932160 | tf_op jit(solution)/shard_map/all_gather | solution.py:227
  227.5 58.4 %all-gather.18.cloned.1.call-start = ((), (), s32[]{:S(2)}) async-start(), calls=%async_computation.16 | async-start | bytes 3932160 | tf_op jit(solution)/shard_map/all_gather | solution.py:239
  229.4 134.0 %reduce-scatter.24.cloned.1.call-start = ((), (), s32[]{:S(2)}) async-start(), calls=%async_computation.22 | async-start | bytes 2654208 | tf_op jit(solution)/shard_map/reduce_scatter | solution.py:295
  294.2 112.8 %all-gather.16.cloned.1.call-start = ((), (), s32[]{:S(2)}) async-start(), calls=%async_computation.14 | async-start | bytes 1327104 | tf_op jit(solution)/shard_map/all_gather | solution.py:197
  365.6 112.9 %reduce-scatter.16.cloned.1.call-start = ((), (), s32[]{:S(2)}) async-start(), calls=%async_computation.17 | async-start | bytes 7864320 | tf_op jit(solution)/shard_map/reduce_scatter | solution.py:247
  421.7 97.1 %reduce-scatter.14.cloned.1.call-start = ((), (), s32[]{:S(2)}) async-start(), calls=%async_computation.15 | async-start | bytes 3932160 | tf_op jit(solution)/shard_map/reduce_scatter | solution.py:233
  431.5 121.3 %all-gather.20.cloned.1.call-start = ((), (), s32[]{:S(2)}) async-start(), calls=%async_computation.18 | async-start | bytes 3932160 | tf_op jit(solution)/shard_map/all_gather | solution.py:256
  524.1 247.2 %reduce-scatter.22.cloned.1.call-start = ((), (), s32[]{:S(2)}) async-start(), calls=%async_computation.21 | async-start | bytes 2654208 | tf_op jit(solution)/shard_map/reduce_scatter | solution.py:294
  536.3 276.4 %reduce-scatter.28.cloned.1.call-start = ((), (), s32[]{:S(2)}) async-start(), calls=%async_computation.24 | async-start | bytes 884736
  750.0 134.2 %reduce-scatter.20.cloned.1.call-start = ((), (), s32[]{:S(2)}) async-start(), calls=%async_computation.20 | async-start | bytes 2654208 | tf_op jit(solution)/shard_map/reduce_scatter | solution.py:292
  758.9 263.2 %reduce-scatter.26.cloned.1.call-start = ((), (), s32[]{:S(2)}) async-start(), calls=%async_computation.23 | async-start | bytes 2162688 | tf_op jit(solution)/shard_map/reduce_scatter | solution.py:297
  763.8 294.8 %reduce-scatter.18.cloned.1.call-start = ((), (), s32[]{:S(2)}) async-start(), calls=%async_computation.19 | async-start | bytes 3932160 | tf_op jit(solution)/shard_map/reduce_scatter | solution.py:281
  814.6 244.0 %copy-start.42 = (f32[512]{0:T(512)S(1)}, f32[512]{0:T(512)}, u32[]{:S(2)}) copy-start(f32[512]{0:T(512)} %copy-done.41) | copy-start | bytes 6148
  (61 other events, 3041.3 us)
Sparse Core Ops, SparseCore 0:
  11.7 61.8 all-gather.9
  75.7 27.2 all-gather.7
  166.3 58.4 reduce-scatter.11
  524.2 28.5 all-gather.19
Sparse Core Ops, SparseCore 1:
  169.4 41.5 all-gather.13
  227.6 28.3 all-gather.11
  257.5 28.3 all-gather.17
  294.3 69.0 reduce-scatter.23
  366.4 40.6 all-gather.15
  421.8 56.7 reduce-scatter.15
  480.9 37.8 reduce-scatter.13
  536.4 69.0 reduce-scatter.21
  750.1 62.6 reduce-scatter.27
  816.3 67.9 reduce-scatter.19
  886.4 135.7 reduce-scatter.25
  1024.8 33.7 reduce-scatter.17
